TPU v7x, 32 devices: a whole 2x2x4 slice. The times are simulated.
32 devices in a mesh: groups: 2 (over x), tok: 8 (over z, y), head: 2 (over core).
Axes of the slice: x: 2, y: 2, z: 4, core: 2. Of those that a mesh axis runs over, the one named last changes fastest.
Arguments:
- video_query: bfloat16 [2, 4096, 4096], P('groups', ('tok', 'head')), parts along dimension 0, may hold values from -640 to 640
- video_key: bfloat16 [2, 4096, 4096], P('groups', ('tok', 'head')), parts along dimension 0, may hold values from -6 to 6
- video_value: bfloat16 [2, 4096, 4096], P('groups', ('tok', 'head')), parts along dimension 0, may hold values from -6 to 6
- audio_query: bfloat16 [2, 1024, 2048], P('groups', ('tok', 'head')), parts along dimension 0, may hold values from -640 to 640
- audio_key: bfloat16 [2, 1024, 2048], P('groups', ('tok', 'head')), parts along dimension 0, may hold values from -6 to 6
- audio_value: bfloat16 [2, 1024, 2048], P('groups', ('tok', 'head')), parts along dimension 0, may hold values from -6 to 6
- cross_audio_query: bfloat16 [2, 1024, 2048], P('groups', ('tok', 'head')), parts along dimension 0, may hold values from -640 to 640
- cross_video_key: bfloat16 [2, 4096, 2048], P('groups', ('tok', 'head')), parts along dimension 0, may hold values from -6 to 6
- cross_video_value: bfloat16 [2, 4096, 2048], P('groups', ('tok', 'head')), parts along dimension 0, may hold values from -6 to 6
- cross_video_query: bfloat16 [2, 4096, 2048], P('groups', ('tok', 'head')), parts along dimension 0, may hold values from -640 to 640
- cross_audio_key: bfloat16 [2, 1024, 2048], P('groups', ('tok', 'head')), parts along dimension 0, may hold values from -6 to 6
- cross_audio_value: bfloat16 [2, 1024, 2048], P('groups', ('tok', 'head')), parts along dimension 0, may hold values from -6 to 6
- audio_frames: int32 [2, 1024], P('groups', ('tok', 'head')), parts along dimension 0, may hold values from 0 to 15
- into_audio_slope: float32 [32], replicated, may hold values from 0.05 to 0.5
- into_video_slope: float32 [32], replicated, may hold values from 0.05 to 0.5
- timestep: int32 [2], P('groups'), parts along dimension 0, may hold values from 0 to 63
- video_gate: bfloat16 [64, 4096], replicated, may hold values from 2 to 12
- audio_gate: bfloat16 [64, 2048], replicated, may hold values from 2 to 12
- into_audio_gate: bfloat16 [64, 2048], replicated, may hold values from 2 to 12
- into_video_gate: bfloat16 [64, 2048], replicated, may hold values from 2 to 12
Outputs:
- video_self: bfloat16 [2, 4096, 4096], P('groups', ('tok', 'head')), parts along dimension 0
- audio_self: bfloat16 [2, 1024, 2048], P('groups', ('tok', 'head')), parts along dimension 0
- audio_cross: bfloat16 [2, 1024, 2048], P('groups', ('tok', 'head')), parts along dimension 0
- video_cross: bfloat16 [2, 4096, 2048], P('groups', ('tok', 'head')), parts along dimension 0
There are 2 independent parts, one for each index of `groups`. A program takes and returns all parts, laid end to end along the dimension named above; an argument that names none is the same for every part. Nothing has to cross between parts.
All inputs are finite; a program needn't handle non-finite values.
Results may differ from a plain program's by a relative error of at most 0.0075.
Values may be sent and summed in bfloat16 or wider, within the bound.
A program may use at most 128 MiB of HBM per device.

v0:
```python
import math

import jax
import jax.numpy as jnp
from jax import lax
from jax.sharding import PartitionSpec as P

LV = 4096
FRAMES = 16
DHV = 128
DHA = 64


def partner(value, axis, stride):
    mask = 2**stride
    pairs = [(source, source ^ mask) for source in range(lax.axis_size(axis))]
    return lax.ppermute(value, axis, pairs)


def split_heads(tensor, head_width):
    samples, counted, columns = tensor.shape
    heads_here = columns // head_width
    return (
        tensor.reshape(samples, counted, heads_here, head_width)
        .transpose(0, 2, 1, 3)
        .reshape(samples * heads_here, counted, head_width)
    )


def join_heads(tensor, samples):
    folded, counted, head_width = tensor.shape
    heads_here = folded // samples
    return (
        tensor.reshape(samples, heads_here, counted, head_width)
        .transpose(0, 2, 1, 3)
        .reshape(samples, counted, heads_here * head_width)
    )


def spread(places, samples, heads_here):
    if places.ndim == 1:
        places = places[None, :]
    counted = places.shape[1]
    return jnp.broadcast_to(places[:, None, :], (samples, heads_here, counted)).reshape(
        samples * heads_here, counted
    )


def lane_rows(which_lane, counted, tok_count, head_count):
    tok_ids = jnp.arange(tok_count, dtype=jnp.int32)[:, None]
    return (tok_ids * head_count + which_lane) * counted + jnp.arange(counted, dtype=jnp.int32)[
        None, :
    ]


def key_order(my_lane, other_lane, counted, tok_count, head_count):
    own_rows = lane_rows(my_lane, counted, tok_count, head_count)
    their_rows = lane_rows(other_lane, counted, tok_count, head_count)
    return jnp.concatenate((own_rows.reshape(-1), their_rows.reshape(-1)))


def attend(queries, keyed, valued, slopes, query_places, key_places):
    folded, counted, head_width = queries.shape
    block_rows = math.gcd(counted, 512)
    blocks_count = counted // block_rows
    score_scale = 1.0 / math.sqrt(head_width)
    query_blocks = queries.reshape(folded, blocks_count, block_rows, head_width).transpose(
        1, 0, 2, 3
    )
    place_blocks = query_places.reshape(folded, blocks_count, block_rows).transpose(1, 0, 2)

    def one_block(packed):
        query_block, place_block = packed
        logit_scores = (
            jnp.einsum("fqd,fkd->fqk", query_block, keyed, preferred_element_type=jnp.float32)
            * score_scale
        )
        if slopes is not None:
            logit_scores = logit_scores - slopes[:, None, None] * jnp.abs(
                place_block[:, :, None] - key_places[:, None, :]
            )
        maxima = jnp.max(logit_scores, axis=2)
        exps = jnp.exp(logit_scores - maxima[:, :, None])
        totals = jnp.sum(exps, axis=2)
        weighted_sum = jnp.einsum(
            "fqk,fkd->fqd", exps.astype(jnp.bfloat16), valued, preferred_element_type=jnp.float32
        )
        return (weighted_sum, maxima, totals)

    weighted_sum, maxima, totals = lax.map(one_block, (query_blocks, place_blocks))
    return (
        weighted_sum.transpose(1, 0, 2, 3).reshape(folded, counted, head_width),
        maxima.transpose(1, 0, 2).reshape(folded, counted),
        totals.transpose(1, 0, 2).reshape(folded, counted),
    )


def finish(partials, gate_values, samples):
    weighted_sum, maxima, totals = partials
    gated = weighted_sum / totals[:, :, None] * gate_values
    return join_heads(gated.astype(jnp.bfloat16), samples)


def on_device(
    video_query,
    video_key,
    video_value,
    audio_query,
    audio_key,
    audio_value,
    cross_audio_query,
    cross_video_key,
    cross_video_value,
    cross_video_query,
    cross_audio_key,
    cross_audio_value,
    audio_frames,
    into_audio_slope,
    into_video_slope,
    timestep,
    video_gate,
    audio_gate,
    into_audio_gate,
    into_video_gate,
):
    samples, video_rows, video_columns = video_query.shape
    audio_rows = audio_query.shape[1]
    tok_count = lax.axis_size("tok")
    head_count = lax.axis_size("head")
    my_lane = lax.axis_index("head")
    other_lane = 1 - my_lane
    head_first = lax.axis_index("tok")
    patches = LV // FRAMES
    audio_times = lax.all_gather(audio_frames, ("tok", "head"), axis=1, tiled=True).astype(
        jnp.float32
    )
    levels = jnp.arange(video_gate.shape[0], dtype=jnp.int32)
    picker = (timestep[:, None] == levels[None, :]).astype(jnp.bfloat16)

    def video_places(row_ids):
        return (row_ids // patches).astype(jnp.float32)

    def audio_places(row_ids):
        return jnp.take(audio_times, row_ids, axis=1)

    def gate_columns(table, head_width, heads_here):
        row_values = jnp.dot(picker, table, preferred_element_type=jnp.float32)
        picked = lax.dynamic_slice_in_dim(
            row_values, head_first * heads_here * head_width, heads_here * head_width, 1
        )
        return picked.reshape(samples * heads_here, 1, head_width)

    def slope_columns(table, heads_here):
        picked = lax.dynamic_slice_in_dim(table, head_first * heads_here, heads_here, 0)
        return picked[None, :].reshape(-1)

    own_video = lane_rows(my_lane, video_rows, tok_count, head_count).reshape(-1)
    own_audio = lane_rows(my_lane, audio_rows, tok_count, head_count).reshape(-1)
    moved = (
        lax.all_to_all(video_query, "tok", split_axis=2, concat_axis=1, tiled=True),
        lax.all_to_all(video_key, "tok", split_axis=2, concat_axis=1, tiled=True),
        lax.all_to_all(video_value, "tok", split_axis=2, concat_axis=1, tiled=True),
        lax.all_to_all(audio_query, "tok", split_axis=2, concat_axis=1, tiled=True),
        lax.all_to_all(audio_key, "tok", split_axis=2, concat_axis=1, tiled=True),
        lax.all_to_all(audio_value, "tok", split_axis=2, concat_axis=1, tiled=True),
        lax.all_to_all(cross_audio_query, "tok", split_axis=2, concat_axis=1, tiled=True),
        lax.all_to_all(cross_video_key, "tok", split_axis=2, concat_axis=1, tiled=True),
        lax.all_to_all(cross_video_value, "tok", split_axis=2, concat_axis=1, tiled=True),
        lax.all_to_all(cross_video_query, "tok", split_axis=2, concat_axis=1, tiled=True),
        lax.all_to_all(cross_audio_key, "tok", split_axis=2, concat_axis=1, tiled=True),
        lax.all_to_all(cross_audio_value, "tok", split_axis=2, concat_axis=1, tiled=True),
    )
    (
        moved_video_query,
        moved_video_key,
        moved_video_value,
        moved_audio_query,
        moved_audio_key,
        moved_audio_value,
        moved_cross_audio_query,
        moved_cross_video_key,
        moved_cross_video_value,
        moved_cross_video_query,
        moved_cross_audio_key,
        moved_cross_audio_value,
    ) = moved
    partner_pieces = partner(
        (
            moved_video_key,
            moved_video_value,
            moved_audio_key,
            moved_audio_value,
            moved_cross_audio_key,
            moved_cross_audio_value,
            moved_cross_audio_query,
        ),
        "head",
        0,
    )
    full_video_key = jnp.concatenate((moved_video_key, partner_pieces[0]), axis=1)
    full_video_value = jnp.concatenate((moved_video_value, partner_pieces[1]), axis=1)
    full_audio_key = jnp.concatenate((moved_audio_key, partner_pieces[2]), axis=1)
    full_audio_value = jnp.concatenate((moved_audio_value, partner_pieces[3]), axis=1)
    full_cross_audio_key = jnp.concatenate((moved_cross_audio_key, partner_pieces[4]), axis=1)
    full_cross_audio_value = jnp.concatenate((moved_cross_audio_value, partner_pieces[5]), axis=1)
    partner_query = partner_pieces[6]
    video_heads = moved_video_query.shape[2] // DHV
    audio_heads = moved_audio_query.shape[2] // DHA
    audio_key_rows = key_order(my_lane, other_lane, audio_rows, tok_count, head_count)
    still_video = jnp.zeros((samples * video_heads, own_video.shape[0]), jnp.float32)
    still_audio = jnp.zeros((samples * audio_heads, own_audio.shape[0]), jnp.float32)
    video_self = finish(
        attend(
            split_heads(moved_video_query, DHV),
            split_heads(full_video_key, DHV),
            split_heads(full_video_value, DHV),
            None,
            still_video,
            None,
        ),
        gate_columns(video_gate, DHV, video_heads),
        samples,
    )
    audio_self = finish(
        attend(
            split_heads(moved_audio_query, DHA),
            split_heads(full_audio_key, DHA),
            split_heads(full_audio_value, DHA),
            None,
            still_audio,
            None,
        ),
        gate_columns(audio_gate, DHA, audio_heads),
        samples,
    )
    video_slopes = slope_columns(into_video_slope, audio_heads)
    video_cross = finish(
        attend(
            split_heads(moved_cross_video_query, DHA),
            split_heads(full_cross_audio_key, DHA),
            split_heads(full_cross_audio_value, DHA),
            video_slopes,
            spread(video_places(own_video), samples, audio_heads),
            spread(audio_places(audio_key_rows), samples, audio_heads),
        ),
        gate_columns(into_video_gate, DHA, audio_heads),
        samples,
    )
    audio_slopes = slope_columns(into_audio_slope, audio_heads)
    own_audio_places = spread(audio_places(own_audio), samples, audio_heads)
    own_keys = split_heads(moved_cross_video_key, DHA)
    own_values = split_heads(moved_cross_video_value, DHA)
    own_key_places = spread(video_places(own_video), samples, audio_heads)
    own_part = attend(
        split_heads(moved_cross_audio_query, DHA),
        own_keys,
        own_values,
        audio_slopes,
        own_audio_places,
        own_key_places,
    )
    partner_audio = lane_rows(other_lane, audio_rows, tok_count, head_count).reshape(-1)
    their_part = attend(
        split_heads(partner_query, DHA),
        own_keys,
        own_values,
        audio_slopes,
        spread(audio_places(partner_audio), samples, audio_heads),
        own_key_places,
    )
    returned = partner((their_part[0], their_part[1], their_part[2]), "head", 0)
    maxima = jnp.maximum(own_part[1], returned[1])
    own_factor = jnp.exp(own_part[1] - maxima)
    their_factor = jnp.exp(returned[1] - maxima)
    merged = (
        own_part[0] * own_factor[:, :, None] + returned[0] * their_factor[:, :, None],
        maxima,
        own_part[2] * own_factor + returned[2] * their_factor,
    )
    audio_cross = finish(merged, gate_columns(into_audio_gate, DHA, audio_heads), samples)
    return (
        lax.all_to_all(video_self, "tok", split_axis=1, concat_axis=2, tiled=True),
        lax.all_to_all(audio_self, "tok", split_axis=1, concat_axis=2, tiled=True),
        lax.all_to_all(audio_cross, "tok", split_axis=1, concat_axis=2, tiled=True),
        lax.all_to_all(video_cross, "tok", split_axis=1, concat_axis=2, tiled=True),
    )


def solution(mesh):
    placed = (
        P("groups", ("tok", "head"), None),
        P("groups", ("tok", "head"), None),
        P("groups", ("tok", "head"), None),
        P("groups", ("tok", "head"), None),
        P("groups", ("tok", "head"), None),
        P("groups", ("tok", "head"), None),
        P("groups", ("tok", "head"), None),
        P("groups", ("tok", "head"), None),
        P("groups", ("tok", "head"), None),
        P("groups", ("tok", "head"), None),
        P("groups", ("tok", "head"), None),
        P("groups", ("tok", "head"), None),
        P("groups", ("tok", "head")),
        P(),
        P(),
        P("groups"),
        P(),
        P(),
        P(),
        P(),
    )
    return jax.shard_map(
        on_device,
        mesh=mesh,
        in_specs=placed,
        out_specs=(
            P("groups", ("tok", "head"), None),
            P("groups", ("tok", "head"), None),
            P("groups", ("tok", "head"), None),
            P("groups", ("tok", "head"), None),
        ),
        check_vma=False,
    )
```

profile of v0, /device:TPU:29, one launch (start us, length us, event | category | flops | bytes accessed | tf_op | source)
XLA Modules:
  0.0 948.4 jit_solution(9676572812332082340)
XLA Ops:
  3.5 11.5 %reduce.4 = bf16[2048,64]{1,0:T(8,128)(2,1)S(1)} reduce(bf16[2048,1,64]{2,1,0:T(2,128)(2,1)S(1)} %bitcast.385, bf16[]{:T(256)} %broadcast.313), dimensions={1}, to_apply=%bitcast.262.reduce_sub_computation | reduce | bytes 524290
  22.3 11.5 %reduce.5 = bf16[2048,64]{1,0:T(8,128)(2,1)S(1)} reduce(bf16[2048,1,64]{2,1,0:T(2,128)(2,1)S(1)} %bitcast.386, bf16[]{:T(256)} %broadcast.313), dimensions={1}, to_apply=%bitcast.264.reduce_sub_computation | reduce | bytes 524290
  41.4 11.5 %reduce.6 = bf16[2048,64]{1,0:T(8,128)(2,1)S(1)} reduce(bf16[2048,1,64]{2,1,0:T(2,128)(2,1)S(1)} %bitcast.387, bf16[]{:T(256)} %broadcast.313), dimensions={1}, to_apply=%bitcast.266.reduce_sub_computation | reduce | bytes 524290
  60.2 11.6 %reduce.8 = bf16[2048,64]{1,0:T(8,128)(2,1)S(1)} reduce(bf16[2048,1,64]{2,1,0:T(2,128)(2,1)S(1)} %bitcast.388, bf16[]{:T(256)} %broadcast.313), dimensions={1}, to_apply=%bitcast.270.reduce_sub_computation | reduce | bytes 524290
  80.9 11.5 %reduce.13 = bf16[2048,64]{1,0:T(8,128)(2,1)S(1)} reduce(bf16[2048,1,64]{2,1,0:T(2,128)(2,1)S(1)} %bitcast.389, bf16[]{:T(256)} %broadcast.313), dimensions={1}, to_apply=%bitcast.280.reduce_sub_computation | reduce | bytes 524290
  99.7 11.5 %reduce.14 = bf16[2048,64]{1,0:T(8,128)(2,1)S(1)} reduce(bf16[2048,1,64]{2,1,0:T(2,128)(2,1)S(1)} %bitcast.390, bf16[]{:T(256)} %broadcast.313), dimensions={1}, to_apply=%bitcast.282.reduce_sub_computation | reduce | bytes 524290
  123.3 11.5 %reduce.9 = bf16[2048,256]{1,0:T(8,128)(2,1)} reduce(bf16[2048,1,256]{2,1,0:T(2,128)(2,1)S(1)} %bitcast.372, bf16[]{:T(256)} %broadcast.313), dimensions={1}, to_apply=%bitcast.272.reduce_sub_computation | reduce | bytes 2097154
  150.3 21.6 %reduce = bf16[4096,256]{1,0:T(8,128)(2,1)S(1)} reduce(bf16[4096,1,256]{2,1,0:T(2,128)(2,1)} %bitcast.355, bf16[]{:T(256)} %broadcast.313), dimensions={1}, to_apply=%bitcast.254.reduce_sub_computation | reduce | bytes 4194306
  185.1 21.6 %reduce.1 = bf16[4096,256]{1,0:T(8,128)(2,1)S(1)} reduce(bf16[4096,1,256]{2,1,0:T(2,128)(2,1)} %bitcast.356, bf16[]{:T(256)} %broadcast.313), dimensions={1}, to_apply=%bitcast.256.reduce_sub_computation | reduce | bytes 4194306
  219.9 21.6 %reduce.2 = bf16[4096,256]{1,0:T(8,128)(2,1)S(1)} reduce(bf16[4096,1,256]{2,1,0:T(2,128)(2,1)} %bitcast.357, bf16[]{:T(256)} %broadcast.313), dimensions={1}, to_apply=%bitcast.258.reduce_sub_computation | reduce | bytes 4194306
  261.2 11.5 %reduce.10 = bf16[2048,256]{1,0:T(8,128)(2,1)} reduce(bf16[2048,1,256]{2,1,0:T(2,128)(2,1)S(1)} %bitcast.373, bf16[]{:T(256)} %broadcast.313), dimensions={1}, to_apply=%bitcast.274.reduce_sub_computation | reduce | bytes 2097154
  294.0 11.5 %reduce.12 = bf16[2048,256]{1,0:T(8,128)(2,1)} reduce(bf16[2048,1,256]{2,1,0:T(2,128)(2,1)S(1)} %bitcast.374, bf16[]{:T(256)} %broadcast.313), dimensions={1}, to_apply=%bitcast.278.reduce_sub_computation | reduce | bytes 2097154
  328.3 13.1 %all-to-all-done.12 = bf16[8,2,32768]{2,1,0:T(2,128)(2,1)S(1)} async-done(((bf16[8,2,32768]{2,1,0:T(2,128)(2,1)}), bf16[8,2,32768]{2,1,0:T(2,128)(2,1)S(1)}, u32[]{:S(2)}, u32[]{:S(2)}) %all-to-all-start.12) | async-done | bytes 1048608 | tf_op jit(solution)/shard_map/all_to_all | solution.py:169
  466.2 28.5 %while.6 = (s32[]{:T(128)}, f32[4,4,512,64]{2,3,1,0:T(8,128)S(1)}, f32[4,4,512]{2,1,0:T(4,128)S(1)}, bf16[4,4,512,64]{2,3,1,0:T(8,128)(2,1)}, bf16[4,1024,64]{1,...) while((s32[]{:T(128)}, f32[4,4,512,64]{2,3,1,0:T(8,128)S(1)}, ...), condition=%wide.region_13.15_spmd.clone, body=%wide.region_10.14_spmd.clone.sunk | while | flops 557838336 | bytes 27078796 | solution.py:90
  543.2 12.8 %reduce.15 = bf16[2048,256]{1,0:T(8,128)(2,1)} reduce(bf16[2048,1,256]{2,1,0:T(2,128)(2,1)} %bitcast.369, bf16[]{:T(256)} %broadcast.313), dimensions={1}, to_apply=%bitcast.284.reduce_sub_computation | reduce | bytes 2097154
  612.6 24.9 %fusion.47 = bf16[1,16384,128]{2,1,0:T(8,128)(2,1)} fusion(bf16[1,2048,512]{2,1,0:T(8,128)(2,1)} %collective-permute-done, bf16[1,2048,512]{2,1,0:T(8,128)(2,1)S(1)} %bitcast.346, bf16[1,4096,128]{2,1,0:T(8,128)(2,1)S(1)} %get-tuple-element.303, bf16[1,4096,128]{2,1,0:T(8,128)(2,1)S(1)} %get-tuple-element.302, bf16[1,4096,128]{2,1,0:T(8,128)(2,1)S(1)} %get-tuple-element.301), kind=kLoop, calls=%fused_computation.63 | loop fusion | flops 20971520 | bytes 11534336 | tf_op jit(solution)/shard_map/concatenate
  646.2 12.7 %fusion.46 = bf16[1,16384,128]{2,1,0:T(8,128)(2,1)} fusion(bf16[1,2048,512]{2,1,0:T(8,128)(2,1)} %copy-done.6, bf16[1,2048,512]{2,1,0:T(8,128)(2,1)S(1)} %bitcast.349, bf16[1,4096,128]{2,1,0:T(8,128)(2,1)} %get-tuple-element.300, bf16[1,4096,128]{2,1,0:T(8,128)(2,1)} %get-tuple-element.299, bf16[1,4096,128]{2,1,0:T(8,128)(2,1)} %get-tuple-element.298), kind=kLoop, calls=%fused_computation.61 | loop fusion | flops 20971520 | bytes 11534336 | tf_op jit(solution)/shard_map/concatenate.1
  664.4 185.7 %while.5 = (s32[]{:T(128)}, f32[4,4,512,128]{3,2,0,1:T(8,128)}, f32[4,4,512]{2,1,0:T(4,128)S(1)}, bf16[4,4,512,128]{3,2,0,1:T(8,128)(2,1)}, bf16[4,4096,128]{2,1...) while((s32[]{:T(128)}, f32[4,4,512,128]{3,2,0,1:T(8,128)}, f32[4,4,512]{2,1,0:T(4,128)S(1)}, ...), condition=%wide.region_3.4_spmd, body=%wide.region_0.3_spmd.sunk | while | flops 4362072064 | bytes 127451264 | solution.py:90
  664.5 18.1 %multiply_reduce_fusion.2 = (f32[4,512]{1,0:T(4,128)S(1)}, f32[4,512,4096]{2,1,0:T(8,128)}) fusion(bf16[4,4096,128]{2,1,0:T(8,128)(2,1)} %get-tuple-element.450, bf16[4,4,512,128]{3,2,0,1:T(8,128)(2,1)} %get-tuple-element.449, s32[]{:T(128)S(6)} %copy.259), kind=kOutput, calls=%fused_computation.5.clone.1 | convolution fusion | flops 2164258816 | bytes 38281220 | tf_op jit(solution)/shard_map/while/body/eval_jaxpr/fqd,fkd->fqk/dot_general | solution.py:75
  682.5 14.3 %fusion.145 = f32[4,4,512,128]{3,2,0,1:T(8,128)} fusion(f32[4,4,512,128]{3,2,0,1:T(8,128)} %get-tuple-element.440, s32[]{:T(128)S(6)} %copy.259, bf16[4,4096,128]{2,1,0:T(8,128)(2,1)S(1)} %copy-done.8, f32[4,512,4096]{2,1,0:T(8,128)} %get-tuple-element.419, f32[4,512]{1,0:T(4,128)S(1)} %get-tuple-element.420), kind=kOutput, calls=%fused_computation.10.clone.1 | convolution fusion | flops 2172649472 | bytes 38805508 | tf_op jit(solution)/shard_map/while/body/eval_jaxpr/fqk,fkd->fqd/dot_general | solution.py:85
  696.8 14.0 %fusion.146 = f32[4,512]{1,0:T(4,128)S(1)} fusion(f32[4,512,4096]{2,1,0:T(8,128)} %get-tuple-element.419, f32[4,512]{1,0:T(4,128)S(1)} %get-tuple-element.420), kind=kLoop, calls=%fused_computation.6.clone.1 | loop fusion | flops 25163776 | bytes 33570816 | tf_op jit(solution)/shard_map/while/body/eval_jaxpr/reduce_sum | solution.py:84
  710.9 18.1 %multiply_reduce_fusion.2 = (f32[4,512]{1,0:T(4,128)S(1)}, f32[4,512,4096]{2,1,0:T(8,128)}) fusion(bf16[4,4096,128]{2,1,0:T(8,128)(2,1)} %get-tuple-element.450, bf16[4,4,512,128]{3,2,0,1:T(8,128)(2,1)} %get-tuple-element.449, s32[]{:T(128)S(6)} %copy.259), kind=kOutput, calls=%fused_computation.5.clone.1 | convolution fusion | flops 2164258816 | bytes 38281220 | tf_op jit(solution)/shard_map/while/body/eval_jaxpr/fqd,fkd->fqk/dot_general | solution.py:75
  729.0 14.3 %fusion.145 = f32[4,4,512,128]{3,2,0,1:T(8,128)} fusion(f32[4,4,512,128]{3,2,0,1:T(8,128)} %get-tuple-element.440, s32[]{:T(128)S(6)} %copy.259, bf16[4,4096,128]{2,1,0:T(8,128)(2,1)S(1)} %copy-done.8, f32[4,512,4096]{2,1,0:T(8,128)} %get-tuple-element.419, f32[4,512]{1,0:T(4,128)S(1)} %get-tuple-element.420), kind=kOutput, calls=%fused_computation.10.clone.1 | convolution fusion | flops 2172649472 | bytes 38805508 | tf_op jit(solution)/shard_map/while/body/eval_jaxpr/fqk,fkd->fqd/dot_general | solution.py:85
  743.3 14.0 %fusion.146 = f32[4,512]{1,0:T(4,128)S(1)} fusion(f32[4,512,4096]{2,1,0:T(8,128)} %get-tuple-element.419, f32[4,512]{1,0:T(4,128)S(1)} %get-tuple-element.420), kind=kLoop, calls=%fused_computation.6.clone.1 | loop fusion | flops 25163776 | bytes 33570816 | tf_op jit(solution)/shard_map/while/body/eval_jaxpr/reduce_sum | solution.py:84
  757.3 18.1 %multiply_reduce_fusion.2 = (f32[4,512]{1,0:T(4,128)S(1)}, f32[4,512,4096]{2,1,0:T(8,128)}) fusion(bf16[4,4096,128]{2,1,0:T(8,128)(2,1)} %get-tuple-element.450, bf16[4,4,512,128]{3,2,0,1:T(8,128)(2,1)} %get-tuple-element.449, s32[]{:T(128)S(6)} %copy.259), kind=kOutput, calls=%fused_computation.5.clone.1 | convolution fusion | flops 2164258816 | bytes 38281220 | tf_op jit(solution)/shard_map/while/body/eval_jaxpr/fqd,fkd->fqk/dot_general | solution.py:75
  775.4 14.3 %fusion.145 = f32[4,4,512,128]{3,2,0,1:T(8,128)} fusion(f32[4,4,512,128]{3,2,0,1:T(8,128)} %get-tuple-element.440, s32[]{:T(128)S(6)} %copy.259, bf16[4,4096,128]{2,1,0:T(8,128)(2,1)S(1)} %copy-done.8, f32[4,512,4096]{2,1,0:T(8,128)} %get-tuple-element.419, f32[4,512]{1,0:T(4,128)S(1)} %get-tuple-element.420), kind=kOutput, calls=%fused_computation.10.clone.1 | convolution fusion | flops 2172649472 | bytes 38805508 | tf_op jit(solution)/shard_map/while/body/eval_jaxpr/fqk,fkd->fqd/dot_general | solution.py:85
  789.7 14.0 %fusion.146 = f32[4,512]{1,0:T(4,128)S(1)} fusion(f32[4,512,4096]{2,1,0:T(8,128)} %get-tuple-element.419, f32[4,512]{1,0:T(4,128)S(1)} %get-tuple-element.420), kind=kLoop, calls=%fused_computation.6.clone.1 | loop fusion | flops 25163776 | bytes 33570816 | tf_op jit(solution)/shard_map/while/body/eval_jaxpr/reduce_sum | solution.py:84
  803.7 18.1 %multiply_reduce_fusion.2 = (f32[4,512]{1,0:T(4,128)S(1)}, f32[4,512,4096]{2,1,0:T(8,128)}) fusion(bf16[4,4096,128]{2,1,0:T(8,128)(2,1)} %get-tuple-element.450, bf16[4,4,512,128]{3,2,0,1:T(8,128)(2,1)} %get-tuple-element.449, s32[]{:T(128)S(6)} %copy.259), kind=kOutput, calls=%fused_computation.5.clone.1 | convolution fusion | flops 2164258816 | bytes 38281220 | tf_op jit(solution)/shard_map/while/body/eval_jaxpr/fqd,fkd->fqk/dot_general | solution.py:75
  821.8 14.3 %fusion.145 = f32[4,4,512,128]{3,2,0,1:T(8,128)} fusion(f32[4,4,512,128]{3,2,0,1:T(8,128)} %get-tuple-element.440, s32[]{:T(128)S(6)} %copy.259, bf16[4,4096,128]{2,1,0:T(8,128)(2,1)S(1)} %copy-done.8, f32[4,512,4096]{2,1,0:T(8,128)} %get-tuple-element.419, f32[4,512]{1,0:T(4,128)S(1)} %get-tuple-element.420), kind=kOutput, calls=%fused_computation.10.clone.1 | convolution fusion | flops 2172649472 | bytes 38805508 | tf_op jit(solution)/shard_map/while/body/eval_jaxpr/fqk,fkd->fqd/dot_general | solution.py:85
  836.1 14.0 %fusion.146 = f32[4,512]{1,0:T(4,128)S(1)} fusion(f32[4,512,4096]{2,1,0:T(8,128)} %get-tuple-element.419, f32[4,512]{1,0:T(4,128)S(1)} %get-tuple-element.420), kind=kLoop, calls=%fused_computation.6.clone.1 | loop fusion | flops 25163776 | bytes 33570816 | tf_op jit(solution)/shard_map/while/body/eval_jaxpr/reduce_sum | solution.py:84
  864.4 14.1 %reduce.3 = bf16[2048,512]{1,0:T(8,128)(2,1)S(1)} reduce(bf16[2048,1,512]{2,1,0:T(2,128)(2,1)} %bitcast.350, bf16[]{:T(256)} %broadcast.313), dimensions={1}, to_apply=%bitcast.260.reduce_sub_computation | reduce | bytes 4194306
  903.0 31.5 %all-to-all-done.3 = bf16[8,2,65536]{2,1,0:T(2,128)(2,1)S(1)} async-done(((bf16[8,2,65536]{2,1,0:T(2,128)(2,1)}), bf16[8,2,65536]{2,1,0:T(2,128)(2,1)S(1)}, u32[]{:S(2)}, u32[]{:S(2)}) %all-to-all-start.3) | async-done | bytes 2097184 | tf_op jit(solution)/shard_map/all_to_all | solution.py:282
  (347 shorter events, 481.9 us)
Async XLA Ops:
  0.6 317.8 %copy-start = (bf16[64,4096]{1,0:T(8,128)(2,1)S(1)}, bf16[64,4096]{1,0:T(8,128)(2,1)}, u32[]{:S(2)}) copy-start(bf16[64,4096]{1,0:T(8,128)(2,1)} %param.42) | copy-start | bytes 1572868
  0.7 39.9 %copy-start.27 = (bf16[1,64,2048]{2,1,0:T(8,128)(2,1)S(1)}, bf16[1,64,2048]{2,1,0:T(8,128)(2,1)}, u32[]{:S(2)}) copy-start(bf16[1,64,2048]{2,1,0:T(8,128)(2,1)} %param.29) | copy-start | bytes 786436
  16.1 18.8 %all-to-all-start.6 = ((bf16[8,2,8192]{2,1,0:T(2,128)(2,1)}), bf16[8,2,8192]{2,1,0:T(2,128)(2,1)S(1)}, u32[]{:S(2)}, u32[]{:S(2)}) async-start(bf16[8,2,8192]{2,1,0:T(2,128)(2,1)} %reshape.520), calls=%async_computation.6 | async-start | bytes 524288 | tf_op jit(solution)/shard_map/all_to_all | solution.py:165
  21.6 37.8 %copy-start.28 = (bf16[1,64,2048]{2,1,0:T(8,128)(2,1)S(1)}, bf16[1,64,2048]{2,1,0:T(8,128)(2,1)}, u32[]{:S(2)}) copy-start(bf16[1,64,2048]{2,1,0:T(8,128)(2,1)} %param.32) | copy-start | bytes 786436
  34.9 19.0 %all-to-all-start.4 = ((bf16[8,2,8192]{2,1,0:T(2,128)(2,1)}), bf16[8,2,8192]{2,1,0:T(2,128)(2,1)S(1)}, u32[]{:S(2)}, u32[]{:S(2)}) async-start(bf16[8,2,8192]{2,1,0:T(2,128)(2,1)} %reshape.522), calls=%async_computation.4 | async-start | bytes 524288 | tf_op jit(solution)/shard_map/all_to_all | solution.py:164
  54.0 39.6 %copy-start.16 = (bf16[8,2,8192]{2,1,0:T(2,128)(2,1)}, bf16[8,2,8192]{2,1,0:T(2,128)(2,1)S(1)}, u32[]{:S(2)}) copy-start(bf16[8,2,8192]{2,1,0:T(2,128)(2,1)S(1)} %all-to-all-done.4) | copy-start | bytes 786436
  54.0 18.8 %all-to-all-start.5 = ((bf16[8,2,8192]{2,1,0:T(2,128)(2,1)}), bf16[8,2,8192]{2,1,0:T(2,128)(2,1)S(1)}, u32[]{:S(2)}, u32[]{:S(2)}) async-start(bf16[8,2,8192]{2,1,0:T(2,128)(2,1)} %reshape.524), calls=%async_computation.5 | async-start | bytes 524288 | tf_op jit(solution)/shard_map/all_to_all | solution.py:163
  60.1 38.8 %copy-start.29 = (bf16[1,64,2048]{2,1,0:T(8,128)(2,1)S(1)}, bf16[1,64,2048]{2,1,0:T(8,128)(2,1)}, u32[]{:S(2)}) copy-start(bf16[1,64,2048]{2,1,0:T(8,128)(2,1)} %param.37) | copy-start | bytes 786436
  72.8 20.7 %all-to-all-start.8 = ((bf16[8,2,8192]{2,1,0:T(2,128)(2,1)}), bf16[8,2,8192]{2,1,0:T(2,128)(2,1)S(1)}, u32[]{:S(2)}, u32[]{:S(2)}) async-start(bf16[8,2,8192]{2,1,0:T(2,128)(2,1)} %reshape.528), calls=%async_computation.8 | async-start | bytes 524288 | tf_op jit(solution)/shard_map/all_to_all | solution.py:166
  93.5 18.8 %all-to-all-start.13 = ((bf16[8,2,8192]{2,1,0:T(2,128)(2,1)}), bf16[8,2,8192]{2,1,0:T(2,128)(2,1)S(1)}, u32[]{:S(2)}, u32[]{:S(2)}) async-start(bf16[8,2,8192]{2,1,0:T(2,128)(2,1)} %reshape.538), calls=%async_computation.13 | async-start | bytes 524288 | tf_op jit(solution)/shard_map/all_to_all | solution.py:170
  113.0 24.2 %all-to-all-start.14 = ((bf16[8,2,8192]{2,1,0:T(2,128)(2,1)}), bf16[8,2,8192]{2,1,0:T(2,128)(2,1)S(1)}, u32[]{:S(2)}, u32[]{:S(2)}) async-start(bf16[8,2,8192]{2,1,0:T(2,128)(2,1)} %reshape.540), calls=%async_computation.14 | async-start | bytes 524288 | tf_op jit(solution)/shard_map/all_to_all | solution.py:171
  137.2 139.0 %all-to-all-start.9 = ((bf16[8,2,32768]{2,1,0:T(2,128)(2,1)}), bf16[8,2,32768]{2,1,0:T(2,128)(2,1)}, u32[]{:S(2)}, u32[]{:S(2)}) async-start(bf16[8,2,32768]{2,1,0:T(2,128)(2,1)} %reshape.530), calls=%async_computation.9 | async-start | bytes 2097152 | tf_op jit(solution)/shard_map/all_to_all | solution.py:167
  276.2 36.9 %all-to-all-start.10 = ((bf16[8,2,32768]{2,1,0:T(2,128)(2,1)}), bf16[8,2,32768]{2,1,0:T(2,128)(2,1)}, u32[]{:S(2)}, u32[]{:S(2)}) async-start(bf16[8,2,32768]{2,1,0:T(2,128)(2,1)} %reshape.532), calls=%async_computation.10 | async-start | bytes 2097152 | tf_op jit(solution)/shard_map/all_to_all | solution.py:168
  313.0 28.4 %all-to-all-start.12 = ((bf16[8,2,32768]{2,1,0:T(2,128)(2,1)}), bf16[8,2,32768]{2,1,0:T(2,128)(2,1)S(1)}, u32[]{:S(2)}, u32[]{:S(2)}) async-start(bf16[8,2,32768]{2,1,0:T(2,128)(2,1)} %reshape.536), calls=%async_computation.12 | async-start | bytes 2097152 | tf_op jit(solution)/shard_map/all_to_all | solution.py:169
  320.8 56.3 %collective-permute-start.3 = (bf16[1,512,256]{2,1,0:T(8,128)(2,1)S(1)}, bf16[1,512,256]{2,1,0:T(8,128)(2,1)}, u32[]{:S(2)}, u32[]{:S(2)}) collective-permute-start(bf16[1,512,256]{2,1,0:T(8,128)(2,1)S(1)} %bitcast.400), channel_id=1, source_target_pairs={{0,1},{1,0},{2,3},{3,2},{4,5},{5,4},{6,7},{7,6},{8,9},{9,8},{10,11... | collective-permute-start | bytes 786440 | tf_op jit(solution)/shard_map/ppermute | solution.py:17
  326.2 52.1 %collective-permute-start.2 = (bf16[1,512,256]{2,1,0:T(8,128)(2,1)S(1)}, bf16[1,512,256]{2,1,0:T(8,128)(2,1)}, u32[]{:S(2)}, u32[]{:S(2)}) collective-permute-start(bf16[1,512,256]{2,1,0:T(8,128)(2,1)S(1)} %bitcast.403), channel_id=1, source_target_pairs={{0,1},{1,0},{2,3},{3,2},{4,5},{5,4},{6,7},{7,6},{8,9},{9,8},{10,11... | collective-permute-start | bytes 786440 | tf_op jit(solution)/shard_map/ppermute | solution.py:17
  342.4 52.5 %all-to-all-start = ((bf16[8,2,65536]{2,1,0:T(2,128)(2,1)}), bf16[8,2,65536]{2,1,0:T(2,128)(2,1)S(1)}, u32[]{:S(2)}, u32[]{:S(2)}) async-start(bf16[8,2,65536]{2,1,0:T(2,128)(2,1)} %reshape.512), calls=%async_computation | async-start | bytes 4194304 | tf_op jit(solution)/shard_map/all_to_all | solution.py:160
  354.9 55.3 %collective-permute-start.4 = (bf16[1,512,256]{2,1,0:T(8,128)(2,1)}, bf16[1,512,256]{2,1,0:T(8,128)(2,1)}, u32[]{:S(2)}, u32[]{:S(2)}) collective-permute-start(bf16[1,512,256]{2,1,0:T(8,128)(2,1)} %bitcast.54), channel_id=1, source_target_pairs={{0,1},{1,0},{2,3},{3,2},{4,5},{5,4},{6,7},{7,6},{8,9},{9,8},{10,11... | collective-permute-start | bytes 786440 | tf_op jit(solution)/shard_map/ppermute | solution.py:17
  370.6 8.9 collective-permute-start.8
  376.5 32.9 %collective-permute-start.9 = (bf16[1,512,256]{2,1,0:T(8,128)(2,1)S(1)}, bf16[1,512,256]{2,1,0:T(8,128)(2,1)S(1)}, u32[]{:S(2)}, u32[]{:S(2)}) collective-permute-start(bf16[1,512,256]{2,1,0:T(8,128)(2,1)S(1)} %bitcast.406), channel_id=1, source_target_pairs={{0,1},{1,0},{2,3},{3,2},{4,5},{5,4},{6,7},{7,6},{8,9},{9,8},{10,11... | collective-permute-start | bytes 786440 | tf_op jit(solution)/shard_map/ppermute | solution.py:17
  394.8 65.3 %all-to-all-start.1 = ((bf16[8,2,65536]{2,1,0:T(2,128)(2,1)}), bf16[8,2,65536]{2,1,0:T(2,128)(2,1)}, u32[]{:S(2)}, u32[]{:S(2)}) async-start(bf16[8,2,65536]{2,1,0:T(2,128)(2,1)} %reshape.514), calls=%async_computation.1 | async-start | bytes 4194304 | tf_op jit(solution)/shard_map/all_to_all | solution.py:161
  432.7 125.4 %collective-permute-start.5 = (f32[4,512]{1,0:T(4,128)S(1)}, f32[4,512]{1,0:T(4,128)S(1)}, u32[]{:S(2)}, u32[]{:S(2)}) collective-permute-start(f32[4,512]{1,0:T(4,128)S(1)} %get-tuple-element.326), channel_id=1, source_target_pairs={{0,1},{1,0},{2,3},{3,2},{4,5},{5,4},{6,7},{7,6},{8,9},{9,8},{10,11... | collective-permute-start | bytes 24584 | tf_op jit(solution)/shard_map/ppermute | solution.py:17
  443.8 114.3 %collective-permute-start.6 = (f32[4,512,64]{1,2,0:T(8,128)}, f32[4,512,64]{1,2,0:T(8,128)S(1)}, u32[]{:S(2)}, u32[]{:S(2)}) collective-permute-start(f32[4,512,64]{1,2,0:T(8,128)} %fusion.35), channel_id=1, source_target_pairs={{0,1},{1,0},{2,3},{3,2},{4,5},{5,4},{6,7},{7,6},{8,9},{9,8},{10,11... | collective-permute-start | bytes 1572872 | tf_op jit(solution)/shard_map/ppermute | solution.py:17
  451.9 106.2 %collective-permute-start.7 = (f32[4,512]{1,0:T(4,128)S(1)}, f32[4,512]{1,0:T(4,128)S(1)}, u32[]{:S(2)}, u32[]{:S(2)}) collective-permute-start(f32[4,512]{1,0:T(4,128)S(1)} %fusion.33), channel_id=1, source_target_pairs={{0,1},{1,0},{2,3},{3,2},{4,5},{5,4},{6,7},{7,6},{8,9},{9,8},{10,11... | collective-permute-start | bytes 24584 | tf_op jit(solution)/shard_map/ppermute | solution.py:17
  460.1 130.1 %all-to-all-start.2 = ((bf16[8,2,65536]{2,1,0:T(2,128)(2,1)}), bf16[8,2,65536]{2,1,0:T(2,128)(2,1)}, u32[]{:S(2)}, u32[]{:S(2)}) async-start(bf16[8,2,65536]{2,1,0:T(2,128)(2,1)} %reshape.516), calls=%async_computation.2 | async-start | bytes 4194304 | tf_op jit(solution)/shard_map/all_to_all | solution.py:162
  517.7 93.1 %collective-permute-start = (bf16[1,2048,512]{2,1,0:T(8,128)(2,1)S(1)}, bf16[1,2048,512]{2,1,0:T(8,128)(2,1)}, u32[]{:S(2)}, u32[]{:S(2)}) collective-permute-start(bf16[1,2048,512]{2,1,0:T(8,128)(2,1)S(1)} %bitcast.344), channel_id=1, source_target_pairs={{0,1},{1,0},{2,3},{3,2},{4,5},{5,4},{6,7},{7,6},{8,9},{9,8},{10,11... | collective-permute-start | bytes 6291464 | tf_op jit(solution)/shard_map/ppermute | solution.py:17
  590.2 50.5 %all-to-all-start.7 = ((bf16[8,2,8192]{2,1,0:T(2,128)(2,1)}), bf16[8,2,8192]{2,1,0:T(2,128)(2,1)S(1)}, u32[]{:S(2)}, u32[]{:S(2)}) async-start(bf16[8,2,8192]{2,1,0:T(2,128)(2,1)} %reshape.526), calls=%async_computation.7 | async-start | bytes 524288 | tf_op jit(solution)/shard_map/all_to_all | solution.py:283
  610.2 27.2 %collective-permute-start.1 = (bf16[1,2048,512]{2,1,0:T(8,128)(2,1)}, bf16[1,2048,512]{2,1,0:T(8,128)(2,1)S(1)}, u32[]{:S(2)}, u32[]{:S(2)}) collective-permute-start(bf16[1,2048,512]{2,1,0:T(8,128)(2,1)} %bitcast.347), channel_id=1, source_target_pairs={{0,1},{1,0},{2,3},{3,2},{4,5},{5,4},{6,7},{7,6},{8,9},{9,8},{10,11... | collective-permute-start | bytes 6291464 | tf_op jit(solution)/shard_map/ppermute | solution.py:17
  640.8 18.2 %all-to-all-start.11 = ((bf16[8,2,8192]{2,1,0:T(2,128)(2,1)}), bf16[8,2,8192]{2,1,0:T(2,128)(2,1)S(1)}, u32[]{:S(2)}, u32[]{:S(2)}) async-start(bf16[8,2,8192]{2,1,0:T(2,128)(2,1)} %reshape.534), calls=%async_computation.11 | async-start | bytes 524288 | tf_op jit(solution)/shard_map/all_to_all | solution.py:284
  659.0 223.3 %all-to-all-start.15 = ((bf16[8,2,32768]{2,1,0:T(2,128)(2,1)}), bf16[8,2,32768]{2,1,0:T(2,128)(2,1)}, u32[]{:S(2)}, u32[]{:S(2)}) async-start(bf16[8,2,32768]{2,1,0:T(2,128)(2,1)} %reshape.542), calls=%async_computation.15 | async-start | bytes 2097152 | tf_op jit(solution)/shard_map/all_to_all | solution.py:285
  664.4 185.7 %copy-start.33 = (f32[4,128]{1,0:T(4,128)S(1)}, f32[4,128]{1,0:T(4,128)}, u32[]{:S(2)}) copy-start(f32[4,128]{1,0:T(4,128)} %dynamic-slice_bitcast_fusion.1) | copy-start | bytes 6148
  882.3 52.2 %all-to-all-start.3 = ((bf16[8,2,65536]{2,1,0:T(2,128)(2,1)}), bf16[8,2,65536]{2,1,0:T(2,128)(2,1)S(1)}, u32[]{:S(2)}, u32[]{:S(2)}) async-start(bf16[8,2,65536]{2,1,0:T(2,128)(2,1)} %reshape.518), calls=%async_computation.3 | async-start | bytes 4194304 | tf_op jit(solution)/shard_map/all_to_all | solution.py:282
  (35 other events, 484.8 us)
where the time goes:
time: 966 us; the launch traced here: 948 us
  other arithmetic  339 us (35%)
  local copies, waits for them, and re-layouts  251 us (26%)
  matrix products  192 us (20%)
  starting transfers between devices  103 us (11%)
  waiting for transfers between devices  50.7 us (5%)
    unnamed x19, other arithmetic  200 us
    unnamed x147, local copies, waits for them, and re-layouts  165 us
    dot_general x11, matrix products, one_block(): jnp.einsum('fqd,fkd->fqk', query_block, keyed, preferred_element_type=jnp...  106 us
    dot_general x11, matrix products, one_block(): jnp.einsum('fqk,fkd->fqd', exps.astype(jnp.bfloat16), valued, preferred_e...  84.6 us
    reduce_sum x11, other arithmetic, one_block(): totals = jnp.sum(exps, axis=2)  81.2 us
    all_to_all x1, waiting for transfers between devices, on_device(): lax.all_to_all(video_self, 'tok', split_axis=1, concat_axis=2, tiled=True)  31.5 us
    concatenate x1, other arithmetic  24.9 us
  transfers between devices with their start and end apart: 26, of which 3 were waited for; matrix products, arithmetic and copies ran while one was open for 79% of the time, Pallas kernels for 0%

commit v1 on v0

--- a/solution.py
+++ b/solution.py
@@ -1,8 +1,11 @@
+import functools
 import math
 
 import jax
 import jax.numpy as jnp
 from jax import lax
+from jax.experimental import pallas as pl
+from jax.experimental.pallas import tpu as pltpu
 from jax.sharding import PartitionSpec as P
 
 LV = 4096
@@ -101,7 +104,7 @@
     return join_heads(gated.astype(jnp.bfloat16), samples)
 
 
-def on_device(
+def by_collectives(
     video_query,
     video_key,
     video_value,
@@ -286,6 +289,315 @@
     )
 
 
+LANES = 128
+LOG2E = 1.4426950408889634
+MESH = pl.DeviceIdType.MESH
+
+
+def softmax_rows(queries, keyed, valued, bias, factor):
+    scores = lax.dot_general(
+        queries, keyed, (((1,), (1,)), ((), ())), preferred_element_type=jnp.float32
+    )
+    if bias is not None:
+        scores = scores - bias
+    maxima = jnp.max(scores, axis=1, keepdims=True)
+    exps = jnp.exp2((scores - maxima) * factor)
+    totals = jnp.sum(exps, axis=1, keepdims=True)
+    summed = jnp.dot(exps.astype(jnp.bfloat16), valued, preferred_element_type=jnp.float32)
+    return summed / totals
+
+
+def kernel(
+    hc, n,
+    vq, vk, vv, aq, ak, av, caq, cvk, cvv, cvq, cak, cav, fr,
+    slope_a, slope_v, gate_v, gate_a, gate_ia, gate_iv,
+    out_vs, out_as, out_ac, out_vc,
+    vqb, vkb, vvb, vob, aqb, akb, avb, aob, caqb, cvkb, cvvb, caob,
+    cvqb, cakb, cavb, cvob, frb, frt,
+    vsend, vrecv, xsend, xrecv, fsend, frecv, vosend, xosend, orecv,
+):
+    me = lax.axis_index("tok") * hc + lax.axis_index("head")
+    rows = vq.shape[1]
+    arows = aq.shape[1]
+    vheads = vqb.shape[0]
+    lv = rows * n
+    la = arows * n
+    patches = lv // FRAMES
+
+    def where(i):
+        return {"tok": i // hc, "head": lax.rem(i, hc)}
+
+    def put(src, dst, send_sem, recv_sem, i):
+        pltpu.make_async_remote_copy(
+            src_ref=src, dst_ref=dst, send_sem=send_sem, recv_sem=recv_sem,
+            device_id=where(i), device_id_type=MESH,
+        ).start()
+
+    def keep(src, dst, sem):
+        pltpu.make_async_copy(src, dst, sem).start()
+
+    def arrived(ref, sem):
+        pltpu.make_async_copy(ref, ref, sem).wait()
+
+    def columns(i, which, each):
+        return pl.ds(pl.multiple_of((i * each + which) * LANES, LANES), LANES)
+
+    vrows = pl.ds(pl.multiple_of(me * rows, rows), rows)
+    myarows = pl.ds(pl.multiple_of(me * arows, arows), arows)
+
+    video = ((vq, vqb), (vk, vkb), (vv, vvb))
+    narrow = (
+        (cvq, cvqb, vrows), (cak, cakb, myarows), (cav, cavb, myarows),
+        (caq, caqb, myarows), (cvk, cvkb, vrows), (cvv, cvvb, vrows),
+        (aq, aqb, myarows), (ak, akb, myarows), (av, avb, myarows),
+    )
+
+    barrier = pltpu.get_barrier_semaphore()
+
+    def greet(j, carry):
+        pl.semaphore_signal(
+            barrier, inc=1, device_id=where(lax.rem(me + j, n)), device_id_type=MESH
+        )
+        return carry
+
+    lax.fori_loop(1, n, greet, 0)
+
+    for h in range(vheads):
+        for at, (src, dst) in enumerate(video):
+            keep(src.at[0, :, columns(me, h, vheads)], dst.at[h, vrows, :], vrecv.at[h, at])
+    for at, (src, dst, here) in enumerate(narrow):
+        keep(src.at[0, :, columns(me, 0, 1)], dst.at[here, :], xrecv.at[at])
+    keep(fr, frb.at[myarows, :], frecv)
+
+    pl.semaphore_wait(barrier, n - 1)
+
+    for h in range(vheads):
+
+        def send_video(j, carry):
+            i = lax.rem(me + j, n)
+            for at, (src, dst) in enumerate(video):
+                put(
+                    src.at[0, :, columns(i, h, vheads)], dst.at[h, vrows, :],
+                    vsend.at[h, at], vrecv.at[h, at], i,
+                )
+            return carry
+
+        lax.fori_loop(1, n, send_video, 0)
+
+    def send_narrow(first, last):
+        def body(j, carry):
+            i = lax.rem(me + j, n)
+            for at in range(first, last):
+                src, dst, here = narrow[at]
+                put(
+                    src.at[0, :, columns(i, 0, 1)], dst.at[here, :],
+                    xsend.at[at], xrecv.at[at], i,
+                )
+            return carry
+
+        lax.fori_loop(1, n, body, 0)
+
+    def send_frames(j, carry):
+        i = lax.rem(me + j, n)
+        put(fr, frb.at[myarows, :], fsend, frecv, i)
+        return carry
+
+    def give(buffer, here, out, cols, send_sem, recv_sem, i):
+        @pl.when(i != me)
+        def _():
+            put(buffer.at[here, :], out.at[0, :, cols], send_sem, recv_sem, i)
+
+        @pl.when(i == me)
+        def _():
+            keep(buffer.at[here, :], out.at[0, :, cols], recv_sem)
+
+    video_factor = LOG2E / math.sqrt(DHV)
+    root = math.sqrt(DHA)
+    narrow_factor = LOG2E / root
+
+    for h in range(vheads):
+        for at, (_, dst) in enumerate(video):
+            arrived(dst.at[h], vrecv.at[h, at])
+        if h == 0:
+            send_narrow(0, 3)
+            lax.fori_loop(1, n, send_frames, 0)
+            send_narrow(3, 9)
+
+        def video_block(j, carry):
+            i = lax.rem(me + 1 + j, n)
+            here = pl.ds(pl.multiple_of(i * rows, rows), rows)
+            part = softmax_rows(vqb[h, here, :], vkb[h], vvb[h], None, video_factor)
+            gated = part * gate_v[:, h * LANES : (h + 1) * LANES]
+            vob[h, here, :] = gated.astype(jnp.bfloat16)
+            give(vob.at[h], here, out_vs, columns(me, h, vheads), vosend.at[h], orecv.at[0], i)
+            return carry
+
+        lax.fori_loop(0, n, video_block, 0)
+
+    lane = lax.broadcasted_iota(jnp.int32, (1, LANES), 1)
+    in_head = [(lane // DHA == h).astype(jnp.float32) for h in range(LANES // DHA)]
+    masks = [mask.astype(jnp.bfloat16) for mask in in_head]
+
+    def both_heads(queries, keyed, valued, biases, gate):
+        total = None
+        for h, mask in enumerate(masks):
+            part = softmax_rows(
+                queries * mask, keyed, valued, biases(h), narrow_factor
+            ) * in_head[h]
+            total = part if total is None else total + part
+        return (total * gate).astype(jnp.bfloat16)
+
+    arrived(frb, frecv)
+    frt[...] = jnp.transpose(frb[...])[0 : frt.shape[0], :]
+
+    for at in range(0, 3):
+        arrived(narrow[at][1], xrecv.at[at])
+
+    def video_cross_block(j, carry):
+        i = lax.rem(me + 1 + j, n)
+        here = pl.ds(pl.multiple_of(i * rows, rows), rows)
+        if patches % rows == 0:
+            places = (i * rows // patches).astype(jnp.float32)
+        else:
+            ids = i * rows + lax.broadcasted_iota(jnp.int32, (rows, 1), 0)
+            places = (ids // patches).astype(jnp.float32)
+        apart = jnp.abs(frt[0:1, :] - places)
+        cvob[here, :] = both_heads(
+            cvqb[here, :], cakb[...], cavb[...], lambda h: apart * (slope_v[h] * root), gate_iv[...]
+        )
+        give(cvob, here, out_vc, columns(me, 0, 1), xosend.at[0], orecv.at[1], i)
+        return carry
+
+    lax.fori_loop(0, n, video_cross_block, 0)
+
+    block = math.gcd(la, 256)
+
+    def give_audio(buffer, out, send_sem, recv_sem):
+        def body(j, carry):
+            i = lax.rem(me + 1 + j, n)
+            here = pl.ds(pl.multiple_of(i * arows, arows), arows)
+            give(buffer, here, out, columns(me, 0, 1), send_sem, recv_sem, i)
+            return carry
+
+        lax.fori_loop(0, n, body, 0)
+
+    for at in range(3, 6):
+        arrived(narrow[at][1], xrecv.at[at])
+
+    def audio_cross_block(b, carry):
+        here = pl.ds(pl.multiple_of(b * block, block), block)
+        key_places = (lax.broadcasted_iota(jnp.int32, (1, lv), 1) // patches).astype(jnp.float32)
+        apart = jnp.abs(frb[here, 0:1] - key_places)
+        caob[here, :] = both_heads(
+            caqb[here, :], cvkb[...], cvvb[...], lambda h: apart * (slope_a[h] * root), gate_ia[...]
+        )
+        return carry
+
+    lax.fori_loop(0, la // block, audio_cross_block, 0)
+    give_audio(caob, out_ac, xosend.at[1], orecv.at[2])
+
+    for at in range(6, 9):
+        arrived(narrow[at][1], xrecv.at[at])
+
+    def audio_self_block(b, carry):
+        here = pl.ds(pl.multiple_of(b * block, block), block)
+        aob[here, :] = both_heads(aqb[here, :], akb[...], avb[...], lambda h: None, gate_a[...])
+        return carry
+
+    lax.fori_loop(0, la // block, audio_self_block, 0)
+    give_audio(aob, out_as, xosend.at[2], orecv.at[3])
+
+    others = n - 1
+    for h in range(vheads):
+        for at, (src, _) in enumerate(video):
+            arrived(src.at[0, :, pl.ds(0, others * LANES)], vsend.at[h, at])
+        arrived(vob.at[h, pl.ds(0, others * rows), :], vosend.at[h])
+    for at, (src, _, _) in enumerate(narrow):
+        arrived(src.at[0, :, pl.ds(0, others * LANES)], xsend.at[at])
+    arrived(frb.at[pl.ds(0, others * arows), :], fsend)
+    arrived(cvob.at[pl.ds(0, others * rows), :], xosend.at[0])
+    arrived(caob.at[pl.ds(0, others * arows), :], xosend.at[1])
+    arrived(aob.at[pl.ds(0, others * arows), :], xosend.at[2])
+    arrived(out_vs, orecv.at[0])
+    arrived(out_vc, orecv.at[1])
+    arrived(out_ac, orecv.at[2])
+    arrived(out_as, orecv.at[3])
+
+
+def in_kernel(arguments):
+    (
+        vq, vk, vv, aq, ak, av, caq, cvk, cvv, cvq, cak, cav, frames,
+        audio_slopes, video_slopes, timestep, gv, ga, gia, giv,
+    ) = arguments
+    hc = lax.axis_size("head")
+    n = lax.axis_size("tok") * hc
+    me = lax.axis_index("tok") * hc + lax.axis_index("head")
+    rows, arows = vq.shape[1], aq.shape[1]
+    lv, la = rows * n, arows * n
+    vheads = vq.shape[2] // n // LANES
+    heads_here = LANES // DHA
+
+    def gate(table, width):
+        return lax.dynamic_slice(table, (timestep[0], me * width), (1, width)).astype(jnp.float32)
+
+    def slopes(table):
+        return lax.dynamic_slice(table, (me * heads_here,), (heads_here,))
+
+    fr = jnp.broadcast_to(frames.reshape(arows, 1).astype(jnp.float32), (arows, LANES))
+    anywhere = pl.BlockSpec(memory_space=pl.ANY)
+    in_smem = pl.BlockSpec(memory_space=pltpu.SMEM)
+    in_vmem = pl.BlockSpec(memory_space=pltpu.VMEM)
+
+    def held(*shape):
+        return pltpu.VMEM(shape, jnp.bfloat16)
+
+    wide, long, short = held(vheads, lv, LANES), held(lv, LANES), held(la, LANES)
+    dma = pltpu.SemaphoreType.DMA
+    video_self, audio_self, audio_cross, video_cross = pl.pallas_call(
+        functools.partial(kernel, hc, n),
+        out_shape=[
+            jax.ShapeDtypeStruct(vq.shape, jnp.bfloat16),
+            jax.ShapeDtypeStruct(aq.shape, jnp.bfloat16),
+            jax.ShapeDtypeStruct(caq.shape, jnp.bfloat16),
+            jax.ShapeDtypeStruct(cvq.shape, jnp.bfloat16),
+        ],
+        in_specs=[anywhere] * 13 + [in_smem] * 2 + [in_vmem] * 4,
+        out_specs=[anywhere] * 4,
+        scratch_shapes=[
+            wide, wide, wide, wide,
+            short, short, short, short,
+            short, long, long, short,
+            long, short, short, long,
+            pltpu.VMEM((la, LANES), jnp.float32),
+            pltpu.VMEM((8, la), jnp.float32),
+            dma((vheads, 3)), dma((vheads, 3)), dma((9,)), dma((9,)),
+            dma, dma, dma((vheads,)), dma((3,)), dma((4,)),
+        ],
+        compiler_params=pltpu.CompilerParams(
+            collective_id=0, has_side_effects=True, vmem_limit_bytes=56 * 1024 * 1024
+        ),
+    )(
+        vq, vk, vv, aq, ak, av, caq, cvk, cvv, cvq, cak, cav, fr,
+        slopes(audio_slopes), slopes(video_slopes),
+        gate(gv, vheads * LANES), gate(ga, LANES), gate(gia, LANES), gate(giv, LANES),
+    )
+    return video_self, audio_self, audio_cross, video_cross
+
+
+def on_device(*arguments):
+    samples, rows, video_columns = arguments[0].shape
+    arows, audio_columns = arguments[3].shape[1:]
+    n = lax.axis_size("tok") * lax.axis_size("head")
+    fits = (
+        samples == 1
+        and video_columns % (n * DHV) == 0
+        and audio_columns == n * LANES
+        and rows % 16 == 0
+        and arows % 16 == 0
+    )
+    return in_kernel(arguments) if fits else by_collectives(*arguments)
+
+
 def solution(mesh):
     placed = (
         P("groups", ("tok", "head"), None),

time: 966 us -> 350 us (0.36); the launches traced: 948 us -> 350 us
  Pallas kernels: 0 us -> 335 us
  other arithmetic: 339 us -> 4.61 us
  local copies, waits for them, and re-layouts: 251 us -> 8.79 us
  matrix products: 192 us -> 0 us
  starting transfers between devices: 103 us -> 0 us
  waiting for transfers between devices: 50.7 us -> 0 us
    pallas_call x0 -> x1, Pallas kernels: none -> 335 us  [in_kernel(): pl.pallas_call(functools.partial(kernel, hc, n), out_shape=[jax.ShapeDtyp...]
    unnamed x19 -> x0, other arithmetic: 200 us -> none
    dot_general x26 -> x0, matrix products: 192 us -> none  [the longest x11 106 us: one_block(): jnp.einsum('fqd,fkd->fqk', query_block, keyed, preferred_element_type=jnp...]
    unnamed x147 -> x10, local copies, waits for them, and re-layouts: 165 us -> 5.63 us
    all_to_all x16 -> x0, starting transfers between devices: 92.4 us -> none  [the longest x1 8.61 us: on_device(): lax.all_to_all(cross_video_value, 'tok', split_axis=2, concat_axis=1, til...]
    reduce_sum x11 -> x0, other arithmetic: 81.2 us -> none  [one_block(): totals = jnp.sum(exps, axis=2)]
    all_to_all x16 -> x0, waiting for transfers between devices: 50.7 us -> none  [the longest x1 31.5 us: on_device(): lax.all_to_all(video_self, 'tok', split_axis=1, concat_axis=2, tiled=True)]
    all_to_all x29 -> x0, local copies, waits for them, and re-layouts: 33.7 us -> none  [the longest x3 6.15 us: on_device(): lax.all_to_all(audio_query, 'tok', split_axis=2, concat_axis=1, tiled=True)]
  transfers between devices with their start and end apart: 26 -> 0, of which waited for: 3 -> 0; matrix products, arithmetic and copies ran while one was open for 79% -> 0% of each run, Pallas kernels for 0% -> 0%
where the time goes in v1:
time: 350 us
  Pallas kernels  335 us (96%)
  local copies, waits for them, and re-layouts  8.79 us (3%)
  other arithmetic  4.61 us (1%)
    pallas_call x1, Pallas kernels, in_kernel(): pl.pallas_call(functools.partial(kernel, hc, n), out_shape=[jax.ShapeDtyp...  335 us

profile of v1, /device:TPU:29, one launch (start us, length us, event | category | flops | bytes accessed | tf_op | source)
XLA Modules:
  0.0 349.6 jit_solution(8335348506594954915)
XLA Ops:
  1.3 0.7 convert_bitcast_fusion
  1.9 1.2 dynamic_slice.18.slope_a
  3.2 1.2 dynamic_slice.19.slope_v
  4.4 1.3 dynamic-slice_convert_fusion.gate_v
  5.7 1.3 dynamic-slice_convert_fusion.3.gate_a
  7.1 1.3 dynamic-slice_convert_fusion.1
  8.4 0.7 broadcast_in_dim.2.fr
  9.1 334.9 %shard_map.219 = (bf16[1,256,4096]{2,1,0:T(8,128)(2,1)}, bf16[1,64,2048]{2,1,0:T(8,128)(2,1)}, bf16[1,64,2048]{2,1,0:T(8,128)(2,1)}, bf16[1,256,2048]{2,1,0:T(8,128)(2,1)}) custom-call(bf16[1,256,4096]{2,1,0:T(8,128)(2,1)} %vq.1, bf16[1,256,4096]{2,1,0:T(8,128)(2,1)} %vk.1, bf16[1,256,4096]{2,1,0:T(8,128)(2,1)} %vv.1, bf16[1,64,2048]{2,1,0:T(8,128)(2,1)} %aq.1, ...), custom_call_target="tpu_custom_call" | custom-call | tf_op jit(solution)/shard_map/pallas_call | solution.py:556
  344.0 0.0 copy-start.2
  344.0 0.0 copy-start.1
  344.0 0.0 copy-start
  344.0 3.2 copy.29
  347.2 0.0 copy-done.2
  347.2 0.7 copy.30
  347.9 0.0 copy-done.1
  347.9 0.7 copy.31
  348.6 0.0 copy-done
  348.6 1.0 copy.32
Async XLA Ops:
  344.0 3.3 copy-start.2
  344.0 4.0 %copy-start.1 = (bf16[1,64,2048]{2,1,0:T(8,128)(2,1)S(1)}, bf16[1,64,2048]{2,1,0:T(8,128)(2,1)}, u32[]{:S(2)}) copy-start(bf16[1,64,2048]{2,1,0:T(8,128)(2,1)} %get-tuple-element.12) | copy-start | bytes 786436
  344.0 4.7 %copy-start = (bf16[1,256,2048]{2,1,0:T(8,128)(2,1)S(1)}, bf16[1,256,2048]{2,1,0:T(8,128)(2,1)}, u32[]{:S(2)}) copy-start(bf16[1,256,2048]{2,1,0:T(8,128)(2,1)} %get-tuple-element.13) | copy-start | bytes 3145732

commit v2 on v1

--- a/solution.py
+++ b/solution.py
@@ -310,11 +310,11 @@
 def kernel(
     hc, n,
     vq, vk, vv, aq, ak, av, caq, cvk, cvv, cvq, cak, cav, fr,
-    slope_a, slope_v, gate_v, gate_a, gate_ia, gate_iv,
+    slope_a, slope_v, level, table_v, table_a, table_ia, table_iv,
     out_vs, out_as, out_ac, out_vc,
     vqb, vkb, vvb, vob, aqb, akb, avb, aob, caqb, cvkb, cvvb, caob,
-    cvqb, cakb, cavb, cvob, frb, frt,
-    vsend, vrecv, xsend, xrecv, fsend, frecv, vosend, xosend, orecv,
+    cvqb, cakb, cavb, cvob, frb, frt, tvb, tab, tiab, tivb, gvb, gab, giab, givb,
+    vsend, vrecv, xsend, xrecv, gsend, grecv, vosend, xosend, orecv, here_sem,
 ):
     me = lax.axis_index("tok") * hc + lax.axis_index("head")
     rows = vq.shape[1]
@@ -347,7 +347,6 @@
 
     video = ((vq, vqb), (vk, vkb), (vv, vvb))
     narrow = (
-        (cvq, cvqb, vrows), (cak, cakb, myarows), (cav, cavb, myarows),
         (caq, caqb, myarows), (cvk, cvkb, vrows), (cvv, cvvb, vrows),
         (aq, aqb, myarows), (ak, akb, myarows), (av, avb, myarows),
     )
@@ -367,13 +366,63 @@
             keep(src.at[0, :, columns(me, h, vheads)], dst.at[h, vrows, :], vrecv.at[h, at])
     for at, (src, dst, here) in enumerate(narrow):
         keep(src.at[0, :, columns(me, 0, 1)], dst.at[here, :], xrecv.at[at])
-    keep(fr, frb.at[myarows, :], frecv)
+    tables = ((table_v, tvb, gvb), (table_a, tab, gab), (table_ia, tiab, giab), (table_iv, tivb, givb))
+    for at, (src, dst, _) in enumerate(tables):
+        width = dst.shape[1]
+        first = 0 if width == src.shape[1] else pl.multiple_of(me * width, LANES)
+        keep(src.at[:, pl.ds(first, width)], dst, here_sem.at[at])
+    keep(cvq.at[0], cvqb, here_sem.at[4])
+
+    ys = 2
+    zs = n // hc // ys
+    core = lax.axis_index("head")
+    yy = lax.rem(lax.axis_index("tok"), ys)
+    zz = lax.axis_index("tok") // ys
+    shared = ((cak.at[0], cakb), (cav.at[0], cavb), (fr, frb))
+
+    def device(z, y, c):
+        return (z * ys + y) * hc + c
+
+    def block_rows(i):
+        return pl.ds(pl.multiple_of(i * arows, arows), arows)
+
+    def hand(i, own, slot, target):
+        for at, (src, dst) in enumerate(shared):
+            held = dst.at[block_rows(i), :]
+            put(src if own else held, held, gsend.at[at, slot], grecv.at[at, i], target)
+
+    def got(i):
+        for at, (_, dst) in enumerate(shared):
+            arrived(dst.at[block_rows(i), :], grecv.at[at, i])
+
+    def up(z, own=False):
+        @pl.when(zz < zs - 1)
+        def _():
+            hand(device(z, yy, core), own, z, device(zz + 1, yy, core))
+
+    def down(z, own=False):
+        @pl.when(zz > 0)
+        def _():
+            hand(device(z, yy, core), own, zs + z, device(zz - 1, yy, core))
+
+    def across(z, own=False):
+        hand(device(z, yy, core), own, 2 * zs + z, device(zz, 1 - yy, core))
+
+    def beside(z, y, own=False):
+        hand(device(z, y, core), own, 3 * zs + z * ys + y, device(zz, yy, 1 - core))
+
+    for at, (src, dst) in enumerate(shared):
+        keep(src, dst.at[block_rows(me), :], grecv.at[at, me])
 
     pl.semaphore_wait(barrier, n - 1)
 
-    for h in range(vheads):
-
-        def send_video(j, carry):
+    up(zz, True)
+    down(zz, True)
+    across(zz, True)
+    beside(zz, yy, True)
+
+    def send_video(h, first, last):
+        def body(j, carry):
             i = lax.rem(me + j, n)
             for at, (src, dst) in enumerate(video):
                 put(
@@ -382,7 +431,38 @@
                 )
             return carry
 
-        lax.fori_loop(1, n, send_video, 0)
+        lax.fori_loop(first, last, body, 0)
+
+    cuts = [1 + (n - 1) * step // (zs + 1) for step in range(zs + 2)]
+    send_video(0, cuts[0], cuts[1])
+    for s in range(1, zs):
+
+        @pl.when(zz - s >= 0)
+        def _():
+            got(device(zz - s, yy, core))
+            up(zz - s)
+            across(zz - s)
+            beside(zz - s, yy)
+
+        @pl.when(zz + s < zs)
+        def _():
+            got(device(zz + s, yy, core))
+            down(zz + s)
+            across(zz + s)
+            beside(zz + s, yy)
+
+        send_video(0, cuts[s], cuts[s + 1])
+    send_video(0, cuts[zs], cuts[zs + 1])
+    for t in range(zs):
+        z = lax.rem(zz + t, zs)
+        got(device(z, 1 - yy, core))
+        beside(z, 1 - yy)
+    for h in range(1, vheads):
+        send_video(h, 1, n)
+    got(me)
+    for t in range(zs):
+        for y in range(ys):
+            got(device(t, y, 1 - core))
 
     def send_narrow(first, last):
         def body(j, carry):
@@ -397,11 +477,6 @@
 
         lax.fori_loop(1, n, body, 0)
 
-    def send_frames(j, carry):
-        i = lax.rem(me + j, n)
-        put(fr, frb.at[myarows, :], fsend, frecv, i)
-        return carry
-
     def give(buffer, here, out, cols, send_sem, recv_sem, i):
         @pl.when(i != me)
         def _():
@@ -414,25 +489,6 @@
     video_factor = LOG2E / math.sqrt(DHV)
     root = math.sqrt(DHA)
     narrow_factor = LOG2E / root
-
-    for h in range(vheads):
-        for at, (_, dst) in enumerate(video):
-            arrived(dst.at[h], vrecv.at[h, at])
-        if h == 0:
-            send_narrow(0, 3)
-            lax.fori_loop(1, n, send_frames, 0)
-            send_narrow(3, 9)
-
-        def video_block(j, carry):
-            i = lax.rem(me + 1 + j, n)
-            here = pl.ds(pl.multiple_of(i * rows, rows), rows)
-            part = softmax_rows(vqb[h, here, :], vkb[h], vvb[h], None, video_factor)
-            gated = part * gate_v[:, h * LANES : (h + 1) * LANES]
-            vob[h, here, :] = gated.astype(jnp.bfloat16)
-            give(vob.at[h], here, out_vs, columns(me, h, vheads), vosend.at[h], orecv.at[0], i)
-            return carry
-
-        lax.fori_loop(0, n, video_block, 0)
 
     lane = lax.broadcasted_iota(jnp.int32, (1, LANES), 1)
     in_head = [(lane // DHA == h).astype(jnp.float32) for h in range(LANES // DHA)]
@@ -447,28 +503,48 @@
             total = part if total is None else total + part
         return (total * gate).astype(jnp.bfloat16)
 
-    arrived(frb, frecv)
+    for at, (_, dst, row) in enumerate(tables):
+        arrived(dst, here_sem.at[at])
+        levels = lax.broadcasted_iota(jnp.int32, (dst.shape[0], 1), 0)
+        picked = jnp.where(levels == level[0], dst[...].astype(jnp.float32), 0.0)
+        row[0:1, :] = jnp.sum(picked, axis=0, keepdims=True)
+    arrived(cvqb, here_sem.at[4])
     frt[...] = jnp.transpose(frb[...])[0 : frt.shape[0], :]
-
-    for at in range(0, 3):
-        arrived(narrow[at][1], xrecv.at[at])
-
-    def video_cross_block(j, carry):
-        i = lax.rem(me + 1 + j, n)
-        here = pl.ds(pl.multiple_of(i * rows, rows), rows)
+    heads_here = LANES // DHA
+
+    def video_cross_block(p, carry):
+        cols = pl.ds(pl.multiple_of(p * LANES, LANES), LANES)
         if patches % rows == 0:
-            places = (i * rows // patches).astype(jnp.float32)
+            places = (me * rows // patches).astype(jnp.float32)
         else:
-            ids = i * rows + lax.broadcasted_iota(jnp.int32, (rows, 1), 0)
+            ids = me * rows + lax.broadcasted_iota(jnp.int32, (rows, 1), 0)
             places = (ids // patches).astype(jnp.float32)
         apart = jnp.abs(frt[0:1, :] - places)
-        cvob[here, :] = both_heads(
-            cvqb[here, :], cakb[...], cavb[...], lambda h: apart * (slope_v[h] * root), gate_iv[...]
+        cvob[:, cols] = both_heads(
+            cvqb[:, cols], cakb[:, cols], cavb[:, cols],
+            lambda h: apart * (slope_v[p * heads_here + h] * root), givb[0:1, cols],
         )
-        give(cvob, here, out_vc, columns(me, 0, 1), xosend.at[0], orecv.at[1], i)
         return carry
 
     lax.fori_loop(0, n, video_cross_block, 0)
+    keep(cvob, out_vc.at[0], here_sem.at[5])
+
+    for h in range(vheads):
+        for at, (_, dst) in enumerate(video):
+            arrived(dst.at[h], vrecv.at[h, at])
+        if h == 0:
+            send_narrow(0, 6)
+
+        def video_block(j, carry):
+            i = lax.rem(me + 1 + j, n)
+            here = pl.ds(pl.multiple_of(i * rows, rows), rows)
+            part = softmax_rows(vqb[h, here, :], vkb[h], vvb[h], None, video_factor)
+            gated = part * gvb[0:1, h * LANES : (h + 1) * LANES]
+            vob[h, here, :] = gated.astype(jnp.bfloat16)
+            give(vob.at[h], here, out_vs, columns(me, h, vheads), vosend.at[h], orecv.at[0], i)
+            return carry
+
+        lax.fori_loop(0, n, video_block, 0)
 
     block = math.gcd(la, 256)
 
@@ -481,7 +557,7 @@
 
         lax.fori_loop(0, n, body, 0)
 
-    for at in range(3, 6):
+    for at in range(0, 3):
         arrived(narrow[at][1], xrecv.at[at])
 
     def audio_cross_block(b, carry):
@@ -489,23 +565,23 @@
         key_places = (lax.broadcasted_iota(jnp.int32, (1, lv), 1) // patches).astype(jnp.float32)
         apart = jnp.abs(frb[here, 0:1] - key_places)
         caob[here, :] = both_heads(
-            caqb[here, :], cvkb[...], cvvb[...], lambda h: apart * (slope_a[h] * root), gate_ia[...]
+            caqb[here, :], cvkb[...], cvvb[...], lambda h: apart * (slope_a[me * heads_here + h] * root), giab[0:1, :]
         )
         return carry
 
     lax.fori_loop(0, la // block, audio_cross_block, 0)
-    give_audio(caob, out_ac, xosend.at[1], orecv.at[2])
-
-    for at in range(6, 9):
+    give_audio(caob, out_ac, xosend.at[0], orecv.at[1])
+
+    for at in range(3, 6):
         arrived(narrow[at][1], xrecv.at[at])
 
     def audio_self_block(b, carry):
         here = pl.ds(pl.multiple_of(b * block, block), block)
-        aob[here, :] = both_heads(aqb[here, :], akb[...], avb[...], lambda h: None, gate_a[...])
+        aob[here, :] = both_heads(aqb[here, :], akb[...], avb[...], lambda h: None, gab[0:1, :])
         return carry
 
     lax.fori_loop(0, la // block, audio_self_block, 0)
-    give_audio(aob, out_as, xosend.at[2], orecv.at[3])
+    give_audio(aob, out_as, xosend.at[1], orecv.at[2])
 
     others = n - 1
     for h in range(vheads):
@@ -514,14 +590,30 @@
         arrived(vob.at[h, pl.ds(0, others * rows), :], vosend.at[h])
     for at, (src, _, _) in enumerate(narrow):
         arrived(src.at[0, :, pl.ds(0, others * LANES)], xsend.at[at])
-    arrived(frb.at[pl.ds(0, others * arows), :], fsend)
-    arrived(cvob.at[pl.ds(0, others * rows), :], xosend.at[0])
-    arrived(caob.at[pl.ds(0, others * arows), :], xosend.at[1])
-    arrived(aob.at[pl.ds(0, others * arows), :], xosend.at[2])
+    arrived(caob.at[pl.ds(0, others * arows), :], xosend.at[0])
+    arrived(aob.at[pl.ds(0, others * arows), :], xosend.at[1])
+
+    def sent(i, slot):
+        for at, (_, dst) in enumerate(shared):
+            arrived(dst.at[block_rows(i), :], gsend.at[at, slot])
+
+    for z in range(zs):
+
+        @pl.when((z <= zz) & (zz < zs - 1))
+        def _():
+            sent(device(z, yy, core), z)
+
+        @pl.when((z >= zz) & (zz > 0))
+        def _():
+            sent(device(z, yy, core), zs + z)
+
+        sent(device(z, yy, core), 2 * zs + z)
+        for y in range(ys):
+            sent(device(z, y, core), 3 * zs + z * ys + y)
     arrived(out_vs, orecv.at[0])
-    arrived(out_vc, orecv.at[1])
-    arrived(out_ac, orecv.at[2])
-    arrived(out_as, orecv.at[3])
+    arrived(out_ac, orecv.at[1])
+    arrived(out_as, orecv.at[2])
+    arrived(out_vc.at[0], here_sem.at[5])
 
 
 def in_kernel(arguments):
@@ -531,28 +623,21 @@
     ) = arguments
     hc = lax.axis_size("head")
     n = lax.axis_size("tok") * hc
-    me = lax.axis_index("tok") * hc + lax.axis_index("head")
     rows, arows = vq.shape[1], aq.shape[1]
     lv, la = rows * n, arows * n
     vheads = vq.shape[2] // n // LANES
-    heads_here = LANES // DHA
-
-    def gate(table, width):
-        return lax.dynamic_slice(table, (timestep[0], me * width), (1, width)).astype(jnp.float32)
-
-    def slopes(table):
-        return lax.dynamic_slice(table, (me * heads_here,), (heads_here,))
-
     fr = jnp.broadcast_to(frames.reshape(arows, 1).astype(jnp.float32), (arows, LANES))
     anywhere = pl.BlockSpec(memory_space=pl.ANY)
     in_smem = pl.BlockSpec(memory_space=pltpu.SMEM)
-    in_vmem = pl.BlockSpec(memory_space=pltpu.VMEM)
 
     def held(*shape):
         return pltpu.VMEM(shape, jnp.bfloat16)
 
     wide, long, short = held(vheads, lv, LANES), held(lv, LANES), held(la, LANES)
     dma = pltpu.SemaphoreType.DMA
+    across = aq.shape[2]
+    levels = gv.shape[0]
+    widths = (vheads * LANES, LANES, LANES, across)
     video_self, audio_self, audio_cross, video_cross = pl.pallas_call(
         functools.partial(kernel, hc, n),
         out_shape=[
@@ -561,25 +646,26 @@
             jax.ShapeDtypeStruct(caq.shape, jnp.bfloat16),
             jax.ShapeDtypeStruct(cvq.shape, jnp.bfloat16),
         ],
-        in_specs=[anywhere] * 13 + [in_smem] * 2 + [in_vmem] * 4,
+        in_specs=[anywhere] * 13 + [in_smem] * 3 + [anywhere] * 4,
         out_specs=[anywhere] * 4,
         scratch_shapes=[
             wide, wide, wide, wide,
             short, short, short, short,
             short, long, long, short,
-            long, short, short, long,
+            held(rows, across), held(la, across), held(la, across), held(rows, across),
             pltpu.VMEM((la, LANES), jnp.float32),
             pltpu.VMEM((8, la), jnp.float32),
-            dma((vheads, 3)), dma((vheads, 3)), dma((9,)), dma((9,)),
-            dma, dma, dma((vheads,)), dma((3,)), dma((4,)),
+            *[held(levels, width) for width in widths],
+            *[pltpu.VMEM((8, width), jnp.float32) for width in widths],
+            dma((vheads, 3)), dma((vheads, 3)), dma((6,)), dma((6,)),
+            dma((3, 5 * (n // hc // 2))), dma((3, n)), dma((vheads,)), dma((2,)), dma((3,)), dma((6,)),
         ],
         compiler_params=pltpu.CompilerParams(
             collective_id=0, has_side_effects=True, vmem_limit_bytes=56 * 1024 * 1024
         ),
     )(
         vq, vk, vv, aq, ak, av, caq, cvk, cvv, cvq, cak, cav, fr,
-        slopes(audio_slopes), slopes(video_slopes),
-        gate(gv, vheads * LANES), gate(ga, LANES), gate(gia, LANES), gate(giv, LANES),
+        audio_slopes, video_slopes, timestep, gv, ga, gia, giv,
     )
     return video_self, audio_self, audio_cross, video_cross
 
@@ -590,6 +676,8 @@
     n = lax.axis_size("tok") * lax.axis_size("head")
     fits = (
         samples == 1
+        and lax.axis_size("head") == 2
+        and lax.axis_size("tok") % 2 == 0
         and video_columns % (n * DHV) == 0
         and audio_columns == n * LANES
         and rows % 16 == 0

time: 350 us -> 309 us (0.88)
  Pallas kernels: 335 us -> 300 us
  other arithmetic: 4.61 us -> 0.66 us
    pallas_call x1, Pallas kernels: 335 us -> 300 us  [in_kernel(): pl.pallas_call(functools.partial(kernel, hc, n), out_shape=[jax.ShapeDtyp...]
    convert_element_type x3 -> x0, other arithmetic: 3.96 us -> none  [gate(): lax.dynamic_slice(table, (timestep[0], me * width), (1, width))]
where the time goes in v2:
time: 309 us
  Pallas kernels  300 us (97%)
  local copies, waits for them, and re-layouts  6.32 us (2%)
    pallas_call x1, Pallas kernels, in_kernel(): pl.pallas_call(functools.partial(kernel, hc, n), out_shape=[jax.ShapeDtyp...  300 us

profile of v2, /device:TPU:29, one launch (start us, length us, event | category | flops | bytes accessed | tf_op | source)
XLA Modules:
  0.0 308.5 jit_solution(8251982832342648340)
XLA Ops:
  1.3 0.7 convert_bitcast_fusion
  1.9 0.7 broadcast_in_dim.2.fr
  2.6 300.2 %shard_map.219 = (bf16[1,256,4096]{2,1,0:T(8,128)(2,1)}, bf16[1,64,2048]{2,1,0:T(8,128)(2,1)}, bf16[1,64,2048]{2,1,0:T(8,128)(2,1)}, bf16[1,256,2048]{2,1,0:T(8,128)(2,1)}) custom-call(bf16[1,256,4096]{2,1,0:T(8,128)(2,1)} %vq.1, bf16[1,256,4096]{2,1,0:T(8,128)(2,1)} %vk.1, bf16[1,256,4096]{2,1,0:T(8,128)(2,1)} %vv.1, bf16[1,64,2048]{2,1,0:T(8,128)(2,1)} %aq.1, ...), custom_call_target="tpu_custom_call" | custom-call | tf_op jit(solution)/shard_map/pallas_call | solution.py:641
  302.9 0.0 copy-start.2
  302.9 0.0 copy-start.1
  302.9 0.0 copy-start
  302.9 3.2 %copy.29 = bf16[1,256,4096]{2,1,0:T(8,128)(2,1)} copy(bf16[1,256,4096]{2,1,0:T(8,128)(2,1)} %get-tuple-element.8) | data formatting | bytes 4194304
  306.1 0.0 copy-done.2
  306.1 0.7 copy.30
  306.9 0.0 copy-done.1
  306.9 0.7 copy.31
  307.6 0.0 copy-done
  307.6 1.0 copy.32
Async XLA Ops:
  302.9 3.3 %copy-start.2 = (bf16[1,64,2048]{2,1,0:T(8,128)(2,1)S(1)}, bf16[1,64,2048]{2,1,0:T(8,128)(2,1)}, u32[]{:S(2)}) copy-start(bf16[1,64,2048]{2,1,0:T(8,128)(2,1)} %get-tuple-element.9) | copy-start | bytes 786436
  302.9 4.0 %copy-start.1 = (bf16[1,64,2048]{2,1,0:T(8,128)(2,1)S(1)}, bf16[1,64,2048]{2,1,0:T(8,128)(2,1)}, u32[]{:S(2)}) copy-start(bf16[1,64,2048]{2,1,0:T(8,128)(2,1)} %get-tuple-element.10) | copy-start | bytes 786436
  302.9 4.7 %copy-start = (bf16[1,256,2048]{2,1,0:T(8,128)(2,1)S(1)}, bf16[1,256,2048]{2,1,0:T(8,128)(2,1)}, u32[]{:S(2)}) copy-start(bf16[1,256,2048]{2,1,0:T(8,128)(2,1)} %get-tuple-element.11) | copy-start | bytes 3145732

commit v3 on v2

--- a/solution.py
+++ b/solution.py
@@ -533,7 +533,8 @@
         for at, (_, dst) in enumerate(video):
             arrived(dst.at[h], vrecv.at[h, at])
         if h == 0:
-            send_narrow(0, 6)
+            send_narrow(0, 3)
+            send_narrow(3, 6)
 
         def video_block(j, carry):
             i = lax.rem(me + 1 + j, n)

time: 309 us -> 305 us (0.987)
    pallas_call x1, Pallas kernels: 300 us -> 297 us  [in_kernel(): pl.pallas_call(functools.partial(kernel, hc, n), out_shape=[jax.ShapeDtyp...]
where the time goes in v3:
time: 305 us
  Pallas kernels  297 us (97%)
  local copies, waits for them, and re-layouts  6.32 us (2%)
    pallas_call x1, Pallas kernels, in_kernel(): pl.pallas_call(functools.partial(kernel, hc, n), out_shape=[jax.ShapeDtyp...  297 us

profile of v3, /device:TPU:29, one launch (start us, length us, event | category | flops | bytes accessed | tf_op | source)
XLA Modules:
  0.0 305.1 jit_solution(15872442055184353787)
XLA Ops:
  1.3 0.7 convert_bitcast_fusion
  1.9 0.7 broadcast_in_dim.2.fr
  2.6 296.8 %shard_map.219 = (bf16[1,256,4096]{2,1,0:T(8,128)(2,1)}, bf16[1,64,2048]{2,1,0:T(8,128)(2,1)}, bf16[1,64,2048]{2,1,0:T(8,128)(2,1)}, bf16[1,256,2048]{2,1,0:T(8,128)(2,1)}) custom-call(bf16[1,256,4096]{2,1,0:T(8,128)(2,1)} %vq.1, bf16[1,256,4096]{2,1,0:T(8,128)(2,1)} %vk.1, bf16[1,256,4096]{2,1,0:T(8,128)(2,1)} %vv.1, bf16[1,64,2048]{2,1,0:T(8,128)(2,1)} %aq.1, ...), custom_call_target="tpu_custom_call" | custom-call | tf_op jit(solution)/shard_map/pallas_call | solution.py:642
  299.4 0.0 copy-start.2
  299.4 0.0 copy-start.1
  299.5 0.0 copy-start
  299.5 3.2 %copy.29 = bf16[1,256,4096]{2,1,0:T(8,128)(2,1)} copy(bf16[1,256,4096]{2,1,0:T(8,128)(2,1)} %get-tuple-element.8) | data formatting | bytes 4194304
  302.7 0.0 copy-done.2
  302.7 0.7 copy.30
  303.4 0.0 copy-done.1
  303.4 0.7 copy.31
  304.1 0.0 copy-done
  304.1 1.0 copy.32
Async XLA Ops:
  299.4 3.3 %copy-start.2 = (bf16[1,64,2048]{2,1,0:T(8,128)(2,1)S(1)}, bf16[1,64,2048]{2,1,0:T(8,128)(2,1)}, u32[]{:S(2)}) copy-start(bf16[1,64,2048]{2,1,0:T(8,128)(2,1)} %get-tuple-element.9) | copy-start | bytes 786436
  299.4 4.0 %copy-start.1 = (bf16[1,64,2048]{2,1,0:T(8,128)(2,1)S(1)}, bf16[1,64,2048]{2,1,0:T(8,128)(2,1)}, u32[]{:S(2)}) copy-start(bf16[1,64,2048]{2,1,0:T(8,128)(2,1)} %get-tuple-element.10) | copy-start | bytes 786436
  299.5 4.7 %copy-start = (bf16[1,256,2048]{2,1,0:T(8,128)(2,1)S(1)}, bf16[1,256,2048]{2,1,0:T(8,128)(2,1)}, u32[]{:S(2)}) copy-start(bf16[1,256,2048]{2,1,0:T(8,128)(2,1)} %get-tuple-element.11) | copy-start | bytes 3145732
